TPU v7x, 256 devices: a whole 4x4x8 slice. The times are simulated.
256 devices in a mesh: group: 8 (over z_hi, x), ep: 32 (over z_lo, y, core).
Axes of the slice: x: 4, y: 4, z: 8 (z_hi: 2, z_lo: 4; z = z_hi * 4 + z_lo), core: 2. Of those that a mesh axis runs over, the one named last changes fastest.
Arguments:
- activations: bfloat16 [49152, 2560], P(('group', 'ep')), may hold values from -6 to 6
- up_grad: bfloat16 [49152, 2, 1536], P(('group', 'ep')), may hold values from -6 to 6
- gate_weights: float32 [49152, 2], P(('group', 'ep')), may hold values from 0.1 to 1
- route_slot: int32 [49152, 2], P(('group', 'ep')), may hold values from 0 to 3, all different within a row; in each aligned block of 192 rows (0 to 191, 192 to 383, ...) at most 144 rows name the same one
- placement: int32 [8, 4], replicated, may hold values from 0 to 7, as said below
- master: float32 [8, 10240, 1536], P('group', 'ep'), may hold values from -0.125 to 0.125
- moment_one: bfloat16 [8, 10240, 1536], P('group', 'ep'), may hold values from -4 to 4
- moment_two: bfloat16 [8, 10240, 1536], P('group', 'ep'), may hold values from 0.099609375 to 4
Outputs:
- input_grad: bfloat16 [49152, 2560], P(('group', 'ep'))
- master_out: float32 [8, 10240, 1536], P('group', 'ep')
- moment_one_out: bfloat16 [8, 10240, 1536], P('group', 'ep')
- moment_two_out: bfloat16 [8, 10240, 1536], P('group', 'ep')
Inputs may be any that keep to these rules, and one draw needn't show every extreme that they name: `route_slot`: each token names 2 different slots; the tokens of one device name one slot at most 144 times. `placement`: slot c of every group holds an expert e with e % 4 == c; every expert is held by at least one group.
All inputs are finite; a program needn't handle non-finite values.
Results may differ from a plain program's by a relative error of at most 0.02.
Values may be sent and summed in bfloat16 or wider, within the bound.
A program may use at most 192 MiB of HBM per device.

v0:
```python
import jax
import jax.numpy as jnp
from jax import lax
from jax.sharding import PartitionSpec as P

SLOTS = 4
EXPERTS = 8


beta_one = 0.9
beta_two = 0.95
learn_rate = 0.01
decay_rate = 0.1
epsilon = 1e-08
grad_scale = 0.0625


def on_device(
    activations, up_grad, gate_weights, route_slot, placement, master, moment_one, moment_two
):
    ep_count = lax.axis_size("ep")
    shards = ep_count // SLOTS
    tok_rows, top_count = route_slot.shape
    hidden = up_grad.shape[2]
    model_width = activations.shape[1]
    piece_width = model_width // shards
    capacity = 3 * tok_rows // 4
    routes = tok_rows * top_count
    scaled = (gate_weights[:, :, None] * up_grad.astype(jnp.float32)).astype(jnp.bfloat16)
    flat_slot = route_slot.reshape(routes)
    onehot = (flat_slot[:, None] == jnp.arange(SLOTS, dtype=jnp.int32)[None, :]).astype(jnp.int32)
    before = jnp.cumsum(onehot, axis=0) - onehot
    position = jnp.sum(before * onehot, axis=1)
    target = flat_slot * capacity + position
    row_table = (
        jnp.full((SLOTS * capacity,), routes, jnp.int32)
        .at[target]
        .set(jnp.arange(routes, dtype=jnp.int32))
    )
    filled = row_table < routes
    source = jnp.minimum(row_table, routes - 1)
    feat_rows = jnp.where(
        filled[:, None], activations[source // top_count], jnp.zeros((), jnp.bfloat16)
    )
    grad_rows = jnp.where(
        filled[:, None], scaled.reshape(routes, hidden)[source], jnp.zeros((), jnp.bfloat16)
    )
    feat_send = (
        feat_rows.reshape(SLOTS, capacity, shards, piece_width)
        .transpose(0, 2, 1, 3)
        .reshape(ep_count, capacity, piece_width)
    )
    grad_send = jnp.broadcast_to(
        grad_rows.reshape(SLOTS, 1, capacity, hidden), (SLOTS, shards, capacity, hidden)
    ).reshape(ep_count, capacity, hidden)
    feat_recv, grad_recv = (
        lax.all_to_all(feat_send, "ep", split_axis=0, concat_axis=0, tiled=True),
        lax.all_to_all(grad_send, "ep", split_axis=0, concat_axis=0, tiled=True),
    )
    feat_flat = feat_recv.reshape(ep_count * capacity, piece_width)
    grad_flat = grad_recv.reshape(ep_count * capacity, hidden)
    weight_copy = master[0].astype(jnp.bfloat16)
    partial_value = lax.dot_general(
        feat_flat, grad_flat, (((0,), (0,)), ((), ())), preferred_element_type=jnp.float32
    )
    back_flat = lax.dot_general(
        grad_flat, weight_copy, (((1,), (1,)), ((), ())), preferred_element_type=jnp.float32
    ).astype(jnp.bfloat16)
    back_send = back_flat.reshape(ep_count, capacity, piece_width)
    back_home = lax.all_to_all(back_send, "ep", split_axis=0, concat_axis=0, tiled=True)
    merged = (
        back_home.reshape(SLOTS, shards, capacity, piece_width)
        .transpose(0, 2, 1, 3)
        .reshape(SLOTS * capacity, model_width)
    )
    route_rows = merged[target].reshape(tok_rows, top_count, model_width)
    input_grad = jnp.sum(route_rows.astype(jnp.float32), axis=1).astype(jnp.bfloat16)
    my_group = lax.axis_index("group")
    my_slot = lax.axis_index("ep") // shards
    my_expert = placement[my_group, my_slot]
    kind_count = EXPERTS // SLOTS
    my_kind = my_expert // SLOTS
    kind_mask = (jnp.arange(kind_count, dtype=jnp.int32) == my_kind)[:, None, None]
    stacked = jnp.where(kind_mask, partial_value[None], jnp.float32(0.0))
    totals = lax.psum(stacked.astype(jnp.bfloat16), "group").astype(jnp.float32)
    summed = jnp.sum(jnp.where(kind_mask, totals, jnp.float32(0.0)), axis=0)
    gradient = summed * grad_scale
    first_moment = beta_one * moment_one[0].astype(jnp.float32) + (1.0 - beta_one) * gradient
    second_moment = (
        beta_two * moment_two[0].astype(jnp.float32) + (1.0 - beta_two) * gradient * gradient
    )
    update = (
        first_moment
        / (1.0 - beta_one**10)
        / (jnp.sqrt(second_moment / (1.0 - beta_two**10)) + epsilon)
    )
    master_out = master[0] - learn_rate * (update + decay_rate * master[0])
    return (
        input_grad,
        master_out[None],
        first_moment.astype(jnp.bfloat16)[None],
        second_moment.astype(jnp.bfloat16)[None],
    )


def solution(mesh):
    in_specs = (
        P(("group", "ep"), None),
        P(("group", "ep"), None, None),
        P(("group", "ep"), None),
        P(("group", "ep"), None),
        P(),
        P("group", "ep", None),
        P("group", "ep", None),
        P("group", "ep", None),
    )
    out_specs = (
        P(("group", "ep"), None),
        P("group", "ep", None),
        P("group", "ep", None),
        P("group", "ep", None),
    )
    return jax.shard_map(
        on_device, mesh=mesh, in_specs=in_specs, out_specs=out_specs, check_vma=False
    )
```

profile of v0, /device:TPU:6, one launch (start us, length us, event | category | flops | bytes accessed | tf_op | source)
XLA Modules:
  0.0 638.8 jit_solution(1186942115725069533)
XLA Ops:
  11.1 2.9 scatter_custom_fusion
  14.9 2.3 multiply_convert_fusion
  17.7 3.6 gather_fusion
  23.0 5.7 broadcast_in_dim.80
  28.7 9.0 %all-to-all-start = ((bf16[32,144,1536]{2,1,0:T(8,128)(2,1)}), bf16[32,144,1536]{2,1,0:T(8,128)(2,1)}, u32[]{:S(2)}, u32[]{:S(2)}) async-start(bf16[32,144,1536]{2,1,0:T(8,128)(2,1)} %bitcast.53), calls=%async_computation | async-start | bytes 28311552 | tf_op jit(solution)/shard_map/all_to_all | solution.py:58
  37.8 4.2 gather_fusion.2
  42.0 5.0 gather.17
  47.1 2.6 copy_select_fusion
  49.6 303.1 %all-to-all-done = bf16[32,144,1536]{2,1,0:T(8,128)(2,1)} async-done(((bf16[32,144,1536]{2,1,0:T(8,128)(2,1)}), bf16[32,144,1536]{2,1,0:T(8,128)(2,1)}, u32[]{:S(2)}, u32[]{:S(2)}) %all-to-all-start) | async-done | bytes 14155808 | tf_op jit(solution)/shard_map/all_to_all | solution.py:58
  352.7 7.0 %all-to-all-start.2 = ((bf16[32,144,320]{2,1,0:T(8,128)(2,1)}), bf16[32,144,320]{2,1,0:T(8,128)(2,1)S(1)}, u32[]{:S(2)}, u32[]{:S(2)}) async-start(bf16[32,144,320]{2,1,0:T(8,128)(2,1)} %bitcast.10), calls=%async_computation.2 | async-start | bytes 7077888 | tf_op jit(solution)/shard_map/all_to_all | solution.py:57
  363.6 11.9 %convolution_convert_fusion = bf16[4608,320]{0,1:T(8,128)(2,1)} fusion(bf16[4608,1536]{1,0:T(8,128)(2,1)} %bitcast.3, f32[1,320,1536]{2,1,0:T(8,128)} %param.13), kind=kOutput, calls=%fused_computation.4 | convolution fusion | flops 4531814400 | bytes 19070976 | tf_op jit(solution)/shard_map/dot_general | solution.py:66
  375.5 5.5 copy.26
  381.1 58.4 %all-to-all-done.2 = bf16[32,144,320]{2,1,0:T(8,128)(2,1)S(1)} async-done(((bf16[32,144,320]{2,1,0:T(8,128)(2,1)}), bf16[32,144,320]{2,1,0:T(8,128)(2,1)S(1)}, u32[]{:S(2)}, u32[]{:S(2)}) %all-to-all-start.2) | async-done | bytes 2949152 | tf_op jit(solution)/shard_map/all_to_all | solution.py:57
  439.4 1.8 copy-done.2
  441.2 5.9 all-to-all-start.1
  447.1 10.8 %convolution_bitcast_fusion = bf16[320,1536]{1,0:T(8,128)(2,1)S(1)} fusion(bf16[32,144,320]{2,1,0:T(8,128)(2,1)} %copy-done.2, bf16[32,144,1536]{2,1,0:T(8,128)(2,1)} %all-to-all-done), kind=kOutput, calls=%fused_computation.9 | convolution fusion | flops 4529848320 | bytes 18087936 | tf_op jit(solution)/shard_map/dot_general | solution.py:63
  459.7 144.2 %all-reduce.2.cloned.1.call-done = bf16[2,320,1536]{2,1,0:T(8,128)(2,1)} async-done(((bf16[2,320,1536]{2,1,0:T(8,128)(2,1)}), bf16[2,320,1536]{2,1,0:T(8,128)(2,1)}) %all-reduce.2.cloned.1.call-update) | async-done | bytes 1966096 | tf_op jit(solution)/shard_map/psum | solution.py:85
  603.9 2.6 select_reduce_fusion
  606.6 4.1 fusion.2
  610.7 2.5 copy.33
  613.2 5.0 reshape.140
  618.2 3.3 gather_fusion.1
  621.5 4.2 reshape.141
  625.7 6.3 reduce_sum.34
  (39 shorter events, 10.1 us)
Async XLA Ops:
  7.2 30.6 %copy-start = (bf16[192,2560]{1,0:T(8,128)(2,1)S(1)}, bf16[192,2560]{1,0:T(8,128)(2,1)}, u32[]{:S(2)}) copy-start(bf16[192,2560]{1,0:T(8,128)(2,1)} %param.8) | copy-start | bytes 2949124
  28.7 324.0 %all-to-all-start = ((bf16[32,144,1536]{2,1,0:T(8,128)(2,1)}), bf16[32,144,1536]{2,1,0:T(8,128)(2,1)}, u32[]{:S(2)}, u32[]{:S(2)}) async-start(bf16[32,144,1536]{2,1,0:T(8,128)(2,1)} %bitcast.53), calls=%async_computation | async-start | bytes 28311552 | tf_op jit(solution)/shard_map/all_to_all | solution.py:58
  352.7 86.7 %all-to-all-start.2 = ((bf16[32,144,320]{2,1,0:T(8,128)(2,1)}), bf16[32,144,320]{2,1,0:T(8,128)(2,1)S(1)}, u32[]{:S(2)}, u32[]{:S(2)}) async-start(bf16[32,144,320]{2,1,0:T(8,128)(2,1)} %bitcast.10), calls=%async_computation.2 | async-start | bytes 7077888 | tf_op jit(solution)/shard_map/all_to_all | solution.py:57
  439.4 1.8 copy-start.2
  441.2 169.5 %all-to-all-start.1 = ((bf16[32,144,320]{2,1,0:T(8,128)(2,1)}), bf16[32,144,320]{2,1,0:T(8,128)(2,1)S(1)}, u32[]{:S(2)}, u32[]{:S(2)}) async-start(bf16[32,144,320]{2,1,0:T(8,128)(2,1)} %bitcast.5), calls=%async_computation.1 | async-start | bytes 7077888 | tf_op jit(solution)/shard_map/all_to_all | solution.py:70
  447.1 156.8 %all-reduce.2.cloned.1.call-start = ((), (), s32[]{:S(2)}) async-start(), calls=%async_computation.3 | async-start | bytes 3932160 | tf_op jit(solution)/shard_map/psum | solution.py:85
  603.9 2.6 copy-start.3
  603.9 2.6 copy-start.4
  603.9 2.7 copy-start.5
  621.5 10.4 %copy-start.1 = (bf16[192,2560]{1,0:T(8,128)(2,1)S(1)}, bf16[192,2560]{1,0:T(8,128)(2,1)}, u32[]{:S(2)}) copy-start(bf16[192,2560]{1,0:T(8,128)(2,1)} %param.8) | copy-start | bytes 2949124
Sparse Core Ops, SparseCore 0:
  459.8 144.0 all-reduce.1
where the time goes:
time: 649 us; the launch traced here: 639 us
  waiting for transfers between devices  506 us (78%)
  local copies, waits for them, and re-layouts  48.1 us (7%)
  other arithmetic  23.5 us (4%)
  matrix products  22.8 us (4%)
  starting transfers between devices  21.9 us (3%)
  between operations  16.9 us (3%)
    all_to_all x1, waiting for transfers between devices, on_device(): lax.all_to_all(grad_send, 'ep', split_axis=0, concat_axis=0, tiled=True)  303 us
    psum x1, waiting for transfers between devices, on_device(): totals = lax.psum(stacked.astype(jnp.bfloat16), 'group').astype(jnp.float32)  144 us
    all_to_all x1, waiting for transfers between devices, on_device(): lax.all_to_all(feat_send, 'ep', split_axis=0, concat_axis=0, tiled=True)  58.4 us
  transfers between devices with their start and end apart: 4, of which 3 were waited for; matrix products, arithmetic and copies ran while one was open for 8% of the time, Pallas kernels for 0%

commit v1 on v0

v1 whole, which is shorter than its diff:
```python
import functools
from types import SimpleNamespace

import jax
import jax.numpy as jnp
from jax import lax
from jax.experimental import pallas as pl
from jax.experimental.pallas import tpu as pltpu
from jax.sharding import PartitionSpec as P

SLOTS = 4
KIND = 4

beta_one = 0.9
beta_two = 0.95
learn_rate = 0.01
decay_rate = 0.1
epsilon = 1e-08
grad_scale = 0.0625

MESH = pl.DeviceIdType.MESH
F32 = jnp.float32
BF16 = jnp.bfloat16

FULL = SimpleNamespace(ZH=2, X=4, Y=4, K=2, T=192, PW=320, NCH=6, HC=256)


def kernel(
    cfg, feat, scl, place, master, ig_out, grad_out,
    wall, fall, ft, mb, sall, pk, part, rl, rr, fin, x1r, zs, zr, x2s, g2, ba, bs, br,
    ysend, yrecv, csend, crecv, fsend, frecv, bsend, brecv,
    wrs, wrr, wls, wlr, prs, prr, pls, plr,
    x1ss, x1rs, zss, zrs, x2ss, x2rs,
):
    ZH, X, Y, K, T, PW, NCH, HC = (
        cfg.ZH, cfg.X, cfg.Y, cfg.K, cfg.T, cfg.PW, cfg.NCH, cfg.HC
    )
    E = Y * K
    LAST = SLOTS - 1
    XR = PW // X
    g, e = lax.axis_index("group"), lax.axis_index("ep")
    zh, x = g // X, g % X
    z, me = e // E, e % E
    y, k = me // K, me % K

    def plane(peer):
        return (g, z * E + peer)

    def ypeer(dy):
        return ((y + dy) % Y) * K + k

    sib = y * K + (K - 1 - k)
    left, right = (g, e - E), (g, e + E)

    def xpeer(dx):
        return (zh * X + (x + dx) % X, e)

    partner = ((ZH - 1 - zh) * X + x, e)

    def rcopy(src, dst, ss, rs, dev):
        return pltpu.make_async_remote_copy(
            src_ref=src, dst_ref=dst, send_sem=ss, recv_sem=rs, device_id=dev, device_id_type=MESH
        )

    barrier = pltpu.get_barrier_semaphore()

    def greet(dev):
        pl.semaphore_signal(barrier, inc=1, device_id=dev, device_id_type=MESH)

    for d in range(1, E):
        greet(plane((me + d) % E))
    for dx in range(1, X):
        greet(xpeer(dx))
    if ZH > 1:
        greet(partner)

    @pl.when(z > 0)
    def _():
        greet(left)

    @pl.when(z < LAST)
    def _():
        greet(right)

    pl.semaphore_wait(
        barrier,
        E - 1 + X - 1 + ZH - 1
        + jnp.where(z > 0, 1, 0) + jnp.where(z < LAST, 1, 0),
    )

    def y_copy(j, dy):
        return rcopy(scl.at[j], sall.at[j, me], ysend.at[j, dy], yrecv.at[j, dy], plane(ypeer(dy)))

    def y_from(j, dy):
        src = sall.at[j, ypeer(-dy)]
        return rcopy(src, src, ysend.at[j, dy], yrecv.at[j, dy], plane(ypeer(dy)))

    def c_copy(j, dy):
        src = scl.at[j] if dy == 0 else sall.at[j, ypeer(-dy)]
        return rcopy(src, sall.at[j, ypeer(-dy)], csend.at[j, dy], crecv.at[j, dy], plane(sib))

    def c_from(j, dy):
        src = sall.at[j, ((y - dy) % Y) * K + (K - 1 - k)]
        return rcopy(src, src, csend.at[j, dy], crecv.at[j, dy], plane(sib))

    def f_copy(d):
        peer = (me + d) % E
        return rcopy(feat.at[peer], fall.at[me], fsend.at[d], frecv.at[d], plane(peer))

    def f_from(d):
        src = fall.at[(me - d) % E]
        return rcopy(src, src, fsend.at[d], frecv.at[d], plane((me + d) % E))

    def b_copy(d):
        peer = (me + d) % E
        return rcopy(bs.at[peer], br.at[me], bsend.at[d], brecv.at[d], plane(peer))

    def b_from(d):
        src = br.at[(me - d) % E]
        return rcopy(src, src, bsend.at[d], brecv.at[d], plane((me + d) % E))

    def w_right(j, s, slot):
        return rcopy(wall.at[j, slot], wall.at[j, slot], wrs.at[j, s], wrr.at[j, s], right)

    def w_left(j, s, slot):
        return rcopy(wall.at[j, slot], wall.at[j, slot], wls.at[j, s], wlr.at[j, s], left)

    def w_from_left(j, s, slot):
        return rcopy(wall.at[j, slot], wall.at[j, slot], wrs.at[j, s], wrr.at[j, s], left)

    def w_from_right(j, s, slot):
        return rcopy(wall.at[j, slot], wall.at[j, slot], wls.at[j, s], wlr.at[j, s], right)

    def p_right(j, c):
        return rcopy(part.at[j, c], rl.at[j, c - 1], prs.at[j, c], prr.at[j, c], right)

    def p_left(j, c):
        return rcopy(part.at[j, c], rr.at[j, c], pls.at[j, c], plr.at[j, c], left)

    def p_from_left(j, c):
        return rcopy(rl.at[j, c - 1], rl.at[j, c - 1], prs.at[j, c], prr.at[j, c], left)

    def p_from_right(j, c):
        return rcopy(rr.at[j, c], rr.at[j, c], pls.at[j, c], plr.at[j, c], right)

    def xrows(who):
        return pl.ds(pl.multiple_of(who * XR, 16), XR)

    def x1_copy(j, dx):
        return rcopy(
            fin.at[j, xrows((x + dx) % X)], x1r.at[j, x], x1ss.at[j, dx], x1rs.at[j, dx], xpeer(dx)
        )

    def x1_from(j, dx):
        src = x1r.at[j, (x - dx) % X]
        return rcopy(src, src, x1ss.at[j, dx], x1rs.at[j, dx], xpeer(dx))

    def z_copy(j):
        return rcopy(zs.at[j], zr.at[j], zss.at[j], zrs.at[j], partner)

    def x2_copy(j, dx):
        return rcopy(
            x2s.at[j, dx], g2.at[j, xrows(x)], x2ss.at[j, dx], x2rs.at[j, dx], xpeer(dx)
        )

    def x2_from(j, dx):
        src = g2.at[j, xrows((x - dx) % X)]
        return rcopy(src, src, x2ss.at[j, dx], x2rs.at[j, dx], xpeer(dx))

    def send_scaled(j):
        for dy in range(1, Y):
            y_copy(j, dy).start()
        if K > 1:
            c_copy(j, 0).start()

    def send_weights(j):
        @pl.when(z < LAST)
        def _():
            w_right(j, 0, z).start()

        @pl.when(z > 0)
        def _():
            w_left(j, 0, z).start()

    def pass_weights(j, s):
        zm = LAST - z

        @pl.when(z >= s)
        def _():
            w_from_left(j, s - 1, z - s).wait_recv()

        @pl.when((z >= s) & (z < LAST))
        def _():
            w_right(j, s, z - s).start()

        @pl.when(zm >= s)
        def _():
            w_from_right(j, s - 1, z + s).wait_recv()

        @pl.when((zm >= s) & (z > 0))
        def _():
            w_left(j, s, z + s).start()

    def partials(j, ring):
        def pick(b, _):
            for c in range(SLOTS):
                m0 = mb[b, :, (2 * c) * 128:(2 * c + 1) * 128]
                m1 = mb[b, :, (2 * c + 1) * 128:(2 * c + 2) * 128]
                for l in range(HC // 128):
                    cols = slice(l * 128, (l + 1) * 128)
                    pk[ring, c, b, :, cols] = (
                        sall[j, b, 0, :, cols] * m0 + sall[j, b, 1, :, cols] * m1
                    )
            return 0

        lax.fori_loop(0, E, pick, 0)

        def one(c, _):
            part[j, c] = jnp.dot(
                ft[...], pk[ring, c].reshape(E * T, HC), preferred_element_type=F32
            ).astype(BF16)
            return 0

        lax.fori_loop(0, SLOTS, one, 0)

    def reduce_stage(j, s):
        @pl.when(z == s)
        def _():
            for c in range(LAST, s, -1):
                if s > 0:
                    p_from_left(j, c).wait_recv()
                    part[j, c] = (part[j, c].astype(F32) + rl[j, c - 1].astype(F32)).astype(BF16)
                p_right(j, c).start()

        @pl.when(z == LAST - s)
        def _():
            for c in range(0, LAST - s):
                if s > 0:
                    p_from_right(j, c).wait_recv()
                    part[j, c] = (part[j, c].astype(F32) + rr[j, c].astype(F32)).astype(BF16)
                p_left(j, c).start()

    def finish(j):
        for zz in range(SLOTS):
            @pl.when(z == zz)
            def _(zz=zz):
                total = part[j, zz].astype(F32)
                if zz > 0:
                    p_from_left(j, zz).wait_recv()
                    total = total + rl[j, zz - 1].astype(F32)
                if zz < LAST:
                    p_from_right(j, zz).wait_recv()
                    total = total + rr[j, zz].astype(F32)
                fin[j] = total.astype(BF16)

        for dx in range(1, X):
            x1_copy(j, dx).start()

    def kind_of(who):
        return jnp.where(place[zh * X + who, z] >= KIND, 1.0, 0.0).astype(F32)

    def kind_sums(j):
        own = fin[j, xrows(x)].astype(F32)
        weight = kind_of(x)
        one = own * weight
        zero = own * (1.0 - weight)
        for dx in range(1, X):
            x1_from(j, dx).wait_recv()
            who = (x - dx) % X
            weight = kind_of(who)
            got = x1r[j, who].astype(F32)
            one += got * weight
            zero += got * (1.0 - weight)
        zs[j, 0] = zero.astype(BF16)
        zs[j, 1] = one.astype(BF16)
        if ZH > 1:
            z_copy(j).start()

    def spread(j):
        zero, one = zs[j, 0].astype(F32), zs[j, 1].astype(F32)
        if ZH > 1:
            z_copy(j).wait_recv()
            zero += zr[j, 0].astype(F32)
            one += zr[j, 1].astype(F32)
        for dx in range(X):
            weight = kind_of((x + dx) % X)
            chosen = (one * weight + zero * (1.0 - weight)).astype(BF16)
            if dx == 0:
                g2[j, xrows(x)] = chosen
            else:
                x2s[j, dx] = chosen
                x2_copy(j, dx).start()

    def collect(j):
        for dx in range(1, X):
            x2_from(j, dx).wait_recv()
        grad_out[:, pl.ds(pl.multiple_of(j * HC, HC), HC)] = g2[j]

    def back(j, ring):
        def block(b, _):
            total = ba[b]
            for c in range(SLOTS):
                total += lax.dot_general(
                    pk[ring, c, b], wall[j, c], (((1,), (1,)), ((), ())),
                    preferred_element_type=F32,
                )
            ba[b] = total
            return 0

        lax.fori_loop(0, E, block, 0)

    for j in range(NCH):
        wall[j, z] = master[:, j * HC:(j + 1) * HC].astype(BF16)
        if j < 3:
            send_weights(j)
        if j == 0:
            for d in range(1, E):
                f_copy(d).start()
        if j < 2:
            send_scaled(j)

    def own_rows(j, _):
        sall[j, me] = scl[j]
        return 0

    lax.fori_loop(0, NCH, own_rows, 0)
    fall[me] = feat[me]

    def clear(b, _):
        ba[b] = jnp.zeros((T, PW), F32)
        return 0

    lax.fori_loop(0, E, clear, 0)

    for d in range(1, E):
        f_from(d).wait_recv()

    first = (PW // 128) * 128
    spot = lax.broadcasted_iota(jnp.int32, (128, 2 * SLOTS * 128), 0)
    lane = lax.broadcasted_iota(jnp.int32, (128, 2 * SLOTS * 128), 1)
    pick_lane = jnp.where(spot - (PW - first) == lane // 128, 1.0, 0.0).astype(BF16)

    def masks(b, _):
        mb[b] = jnp.dot(
            fall[b, :, first:first + 128], pick_lane, preferred_element_type=F32
        ).astype(BF16)
        return 0

    lax.fori_loop(0, E, masks, 0)
    ft[...] = fall[...].reshape(E * T, fall.shape[2]).T[:PW]

    def when_chunk(i, lag, f):
        j = i - lag

        @pl.when((j >= 0) & (j < NCH))
        def _():
            f(j)

    def step(i, _):
        def gather(j):
            for dy in range(1, Y):
                y_from(j, dy).wait_recv()
                if K > 1:
                    c_copy(j, dy).start()

        when_chunk(i, 0, gather)
        when_chunk(i, -2, send_scaled)
        when_chunk(i, 0, lambda j: pass_weights(j, 1))
        when_chunk(i, 1, lambda j: pass_weights(j, 2))
        when_chunk(i, 2, lambda j: pass_weights(j, 3))
        when_chunk(i, -3, send_weights)

        def compute(j):
            if K > 1:
                for dy in range(Y):
                    c_from(j, dy).wait_recv()
            partials(j, j % 3)
            reduce_stage(j, 0)

        when_chunk(i, 0, compute)
        when_chunk(i, 1, lambda j: reduce_stage(j, 1))
        when_chunk(i, 2, lambda j: reduce_stage(j, 2))
        when_chunk(i, 3, finish)
        when_chunk(i, 4, kind_sums)
        when_chunk(i, 5, spread)
        when_chunk(i, 6, collect)
        when_chunk(i, 2, lambda j: back(j, j % 3))

        @pl.when(i == NCH + 1)
        def _():
            def out(b, _):
                bs[b] = ba[b].astype(BF16)
                return 0

            lax.fori_loop(0, E, out, 0)
            for d in range(1, E):
                b_copy(d).start()

        return 0

    lax.fori_loop(0, NCH + 7, step, 0)

    br[me] = bs[me]
    for d in range(1, E):
        b_from(d).wait_recv()
    ig_out[...] = br[...]

    for d in range(1, E):
        f_copy(d).wait_send()
        b_copy(d).wait_send()

    def drain(j, _):
        for dy in range(1, Y):
            y_copy(j, dy).wait_send()
        if K > 1:
            for dy in range(Y):
                c_copy(j, dy).wait_send()
        for s in range(SLOTS - 1):
            @pl.when((z >= s) & (z < LAST))
            def _(s=s):
                w_right(j, s, z - s).wait_send()

            @pl.when((LAST - z >= s) & (z > 0))
            def _(s=s):
                w_left(j, s, z + s).wait_send()

            @pl.when(z == s)
            def _(s=s):
                for c in range(LAST, s, -1):
                    p_right(j, c).wait_send()

            @pl.when(z == LAST - s)
            def _(s=s):
                for c in range(0, LAST - s):
                    p_left(j, c).wait_send()

        for dx in range(1, X):
            x1_copy(j, dx).wait_send()
            x2_copy(j, dx).wait_send()
        if ZH > 1:
            z_copy(j).wait_send()
        return 0

    lax.fori_loop(0, NCH, drain, 0)


def exchange(cfg, feat, scl, place, master):
    ZH, X, Y, K, T, PW, NCH, HC = (
        cfg.ZH, cfg.X, cfg.Y, cfg.K, cfg.T, cfg.PW, cfg.NCH, cfg.HC
    )
    E = Y * K
    PWL = feat.shape[2]
    XR = PW // X
    DMA = pltpu.SemaphoreType.DMA
    vm = pl.BlockSpec(memory_space=pltpu.VMEM)
    sm = pl.BlockSpec(memory_space=pltpu.SMEM)

    def sems(*shape):
        return [DMA(shape), DMA(shape)]

    return pl.pallas_call(
        functools.partial(kernel, cfg),
        out_shape=(
            jax.ShapeDtypeStruct((E, T, PW), BF16),
            jax.ShapeDtypeStruct((PW, NCH * HC), BF16),
        ),
        in_specs=[vm, vm, sm, vm],
        out_specs=(vm, vm),
        scratch_shapes=[
            pltpu.VMEM((NCH, SLOTS, PW, HC), BF16),
            pltpu.VMEM((E, T, PWL), BF16),
            pltpu.VMEM((PW, E * T), BF16),
            pltpu.VMEM((E, T, 2 * SLOTS * 128), BF16),
            pltpu.VMEM((NCH, E, 2, T, HC), BF16),
            pltpu.VMEM((3, SLOTS, E, T, HC), BF16),
            pltpu.VMEM((NCH, SLOTS, PW, HC), BF16),
            pltpu.VMEM((NCH, SLOTS - 1, PW, HC), BF16),
            pltpu.VMEM((NCH, SLOTS - 1, PW, HC), BF16),
            pltpu.VMEM((NCH, PW, HC), BF16),
            pltpu.VMEM((NCH, X, XR, HC), BF16),
            pltpu.VMEM((NCH, 2, XR, HC), BF16),
            pltpu.VMEM((NCH, 2, XR, HC), BF16),
            pltpu.VMEM((NCH, X, XR, HC), BF16),
            pltpu.VMEM((NCH, PW, HC), BF16),
            pltpu.VMEM((E, T, PW), F32),
            pltpu.VMEM((E, T, PW), BF16),
            pltpu.VMEM((E, T, PW), BF16),
            *sems(NCH, Y), *sems(NCH, Y), *sems(E), *sems(E),
            *sems(NCH, SLOTS), *sems(NCH, SLOTS), *sems(NCH, SLOTS), *sems(NCH, SLOTS),
            *sems(NCH, X), *sems(NCH), *sems(NCH, X),
        ],
        compiler_params=pltpu.CompilerParams(
            collective_id=0, has_side_effects=True, vmem_limit_bytes=62 << 20
        ),
        name="exchange",
    )(feat, scl, place, master)


def on_device(
    cfg, activations, up_grad, gate_weights, route_slot, placement, master, moment_one, moment_two
):
    E, T, PW, NCH, HC = cfg.Y * cfg.K, cfg.T, cfg.PW, cfg.NCH, cfg.HC
    scaled = (gate_weights[:, :, None] * up_grad.astype(F32)).astype(BF16)
    scl = scaled.reshape(T, 2, NCH, HC).transpose(2, 1, 0, 3)
    pad = -PW % 128
    onehot = (
        route_slot[:, None, :] == jnp.arange(SLOTS, dtype=jnp.int32)[None, :, None]
    ).reshape(T, 2 * SLOTS).astype(BF16)
    marks = jnp.pad(onehot, ((0, 0), (0, pad - 2 * SLOTS)))
    feat = jnp.concatenate(
        [
            activations.reshape(T, E, PW).transpose(1, 0, 2),
            jnp.broadcast_to(marks[None], (E, T, pad)),
        ],
        axis=2,
    )
    back, grad = exchange(cfg, feat, scl, placement, master[0])
    input_grad = back.transpose(1, 0, 2).reshape(T, E * PW)
    gradient = grad.astype(F32) * grad_scale
    first_moment = beta_one * moment_one[0].astype(F32) + (1.0 - beta_one) * gradient
    second_moment = (
        beta_two * moment_two[0].astype(F32) + (1.0 - beta_two) * gradient * gradient
    )
    update = (
        first_moment
        / (1.0 - beta_one**10)
        / (jnp.sqrt(second_moment / (1.0 - beta_two**10)) + epsilon)
    )
    master_out = master[0] - learn_rate * (update + decay_rate * master[0])
    return (
        input_grad,
        master_out[None],
        first_moment.astype(BF16)[None],
        second_moment.astype(BF16)[None],
    )


def solution(mesh, cfg=FULL):
    in_specs = (
        P(("group", "ep"), None),
        P(("group", "ep"), None, None),
        P(("group", "ep"), None),
        P(("group", "ep"), None),
        P(),
        P("group", "ep", None),
        P("group", "ep", None),
        P("group", "ep", None),
    )
    out_specs = (
        P(("group", "ep"), None),
        P("group", "ep", None),
        P("group", "ep", None),
        P("group", "ep", None),
    )
    return jax.shard_map(
        functools.partial(on_device, cfg),
        mesh=mesh, in_specs=in_specs, out_specs=out_specs, check_vma=False,
    )
```

time: 649 us -> 173 us (0.27); the launches traced: 639 us -> 170 us
  waiting for transfers between devices: 506 us -> 0 us
  Pallas kernels: 0 us -> 149 us
  local copies, waits for them, and re-layouts: 48.1 us -> 10 us
  matrix products: 22.8 us -> 0 us
  starting transfers between devices: 21.9 us -> 0 us
  between operations: 16.9 us -> 0.71 us
  other arithmetic: 23.5 us -> 9.63 us
    all_to_all x3 -> x0, waiting for transfers between devices: 361 us -> none  [the longest x1 303 us: on_device(): lax.all_to_all(grad_send, 'ep', split_axis=0, concat_axis=0, tiled=True)]
    pallas_call x0 -> x1, Pallas kernels: none -> 149 us  [exchange(): pl.pallas_call(functools.partial(kernel, cfg), out_shape=(jax.ShapeDtypeS...]
    psum x1 -> x0, waiting for transfers between devices: 144 us -> none  [on_device(): totals = lax.psum(stacked.astype(jnp.bfloat16), 'group').astype(jnp.float32)]
    dot_general x2 -> x0, matrix products: 22.8 us -> none  [the longest x1 11.9 us: on_device(): lax.dot_general(grad_flat, weight_copy, (((1,), (1,)), ((), ())), preferr...]
    all_to_all x3 -> x0, starting transfers between devices: 21.9 us -> none  [the longest x1 9.04 us: on_device(): lax.all_to_all(grad_send, 'ep', split_axis=0, concat_axis=0, tiled=True)]
    gather x4 -> x0, local copies, waits for them, and re-layouts: 16.2 us -> none  [the longest x2 9.28 us: on_device(): activations[source // top_count]]
    reduce_sum x3 -> x0, other arithmetic: 8.83 us -> none  [the longest x1 6.25 us: on_device(): jnp.sum(route_rows.astype(jnp.float32), axis=1).astype(jnp.bfloat16)]
    reshape x4 -> x5, local copies, waits for them, and re-layouts: 12.2 us -> 4.82 us  [the longest x2 2.23 us: on_device(): scl = scaled.reshape(T, 2, NCH, HC).transpose(2, 1, 0, 3)]
  transfers between devices with their start and end apart: 4 -> 0, of which waited for: 3 -> 0; matrix products, arithmetic and copies ran while one was open for 8% -> 0% of each run, Pallas kernels for 0% -> 0%
where the time goes in v1:
time: 173 us; the launch traced here: 170 us
  Pallas kernels  149 us (86%)
  local copies, waits for them, and re-layouts  10 us (6%)
  other arithmetic  9.63 us (6%)
    pallas_call x1, Pallas kernels, exchange(): pl.pallas_call(functools.partial(kernel, cfg), out_shape=(jax.ShapeDtypeS...  149 us
    broadcast_in_dim x1, other arithmetic, on_device(): second_moment.astype(BF16)[None]  6.01 us

profile of v1, /device:TPU:6, one launch (start us, length us, event | category | flops | bytes accessed | tf_op | source)
XLA Modules:
  0.0 169.6 jit_solution(12372779896392717005)
XLA Ops:
  0.6 0.1 eq.23
  0.7 1.3 copy.20.place
  2.1 0.7 eq.20
  2.8 0.1 broadcast_compare_fusion
  2.9 0.1 copy.16
  3.0 0.8 copy.17
  3.8 0.1 broadcast_in_dim.8
  3.8 2.3 %multiply_convert_fusion = bf16[192,2,1536]{2,1,0:T(2,128)(2,1)S(1)} fusion(bf16[192,2,1536]{2,1,0:T(2,128)(2,1)} %param.9, f32[192,2]{1,0:T(8,128)S(1)} %copy.17), kind=kLoop, calls=%fused_computation.3 | loop fusion | flops 1769472 | bytes 2360832 | tf_op jit(solution)/shard_map/convert_element_type | solution.py:503
  6.1 0.8 reshape.32
  6.9 0.0 copy-start.1
  7.0 1.4 copy.26
  8.4 0.0 copy-done.1
  8.4 0.9 reshape.29
  9.3 0.2 copy.27
  9.4 1.3 pad_maximum_fusion.feat
  10.7 149.2 %exchange.1 = (bf16[8,192,320]{2,1,0:T(8,128)(2,1)}, bf16[320,1536]{1,0:T(8,128)(2,1)}) custom-call(bf16[8,192,384]{2,1,0:T(8,128)(2,1)} %pad_maximum_fusion.feat, bf16[6,2,192,256]{3,2,1,0:T(8,128)(2,1)} %bitcast.34, s32[8,4]{1,0:T(8,128)} %copy.20.place, f32[320,1536]{1,0:T(8,128)} %bitcast.33), custom_call_target="tpu_custom_call" | custom-call | tf_op jit(solution)/shard_map/exchange/pallas_call | solution.py:461
  160.0 0.0 copy-start
  160.0 2.1 %copy.21 = bf16[192,8,320]{2,1,0:T(8,128)(2,1)S(1)} copy(bf16[192,8,320]{2,0,1:T(8,128)(2,1)} %bitcast.36) | data formatting | bytes 1966080 | tf_op jit(solution)/shard_map/transpose | solution.py:518
  162.1 1.5 reshape.31
  163.6 0.0 copy-done
  163.6 6.0 %fusion.5 = (bf16[1,320,1536]{2,1,0:T(8,128)(2,1)}, f32[1,320,1536]{2,1,0:T(8,128)}, bf16[1,320,1536]{2,1,0:T(8,128)(2,1)}) fusion(bf16[320,1536]{1,0:T(8,128)(2,1)} %get-tuple-element.7, bf16[1,320,1536]{2,1,0:T(8,128)(2,1)} %param.15, bf16[1,320,1536]{2,1,0:T(8,128)(2,1)} %param.14, f32[1,320,1536]{2,1,0:T(8,128)S(1)} %copy-done), kind=kLoop, calls=%fused_computation.13 | loop fusion | flops 10321920 | bytes 8847360 | tf_op jit(solution)/shard_map/broadcast_in_dim | solution.py:534
  (3 shorter events, 0.0 us)
Async XLA Ops:
  6.9 1.4 copy-start.1
  160.0 3.7 %copy-start = (f32[1,320,1536]{2,1,0:T(8,128)S(1)}, f32[1,320,1536]{2,1,0:T(8,128)}, u32[]{:S(2)}) copy-start(f32[1,320,1536]{2,1,0:T(8,128)} %param.13) | copy-start | bytes 5898244

commit v2 on v1

v2 whole, which is shorter than its diff:
```python
import functools
from types import SimpleNamespace

import jax
import jax.numpy as jnp
from jax import lax
from jax.experimental import pallas as pl
from jax.experimental.pallas import tpu as pltpu
from jax.sharding import PartitionSpec as P

SLOTS = 4
KIND = 4

beta_one = 0.9
beta_two = 0.95
learn_rate = 0.01
decay_rate = 0.1
epsilon = 1e-08
grad_scale = 0.0625

MESH = pl.DeviceIdType.MESH
F32 = jnp.float32
BF16 = jnp.bfloat16

FULL = SimpleNamespace(ZH=2, X=4, Y=4, K=2, T=192, PW=320, NCH=6, HC=256, RING=3, BACK=2)


def kernel(
    cfg, feat, grads, gates, slots, place, master, mom1, mom2,
    ig_out, master_out, mom1_out, mom2_out,
    fv, uv, mv, v1, v2, gm, fs,
    wall, fall, ft, mb, sall, pk, part, ks, rl, rr, x1r, zs, zr, x2s, g2, ba, bs, br,
    ysend, yrecv, hsend, hrecv, csend, crecv, osend, orecv, fsend, frecv, bsend, brecv,
    wrs, wrr, wls, wlr, prs, prr, pls, plr,
    x1ss, x1rs, zss, zrs, x2ss, x2rs,
    lsem, msem, v1sem, v2sem, mosem, o1sem, o2sem,
):
    ZH, X, Y, K, T, PW, NCH, HC = (
        cfg.ZH, cfg.X, cfg.Y, cfg.K, cfg.T, cfg.PW, cfg.NCH, cfg.HC
    )
    E = Y * K
    LAST = SLOTS - 1
    XR = PW // X
    near = {1: (), 2: (1,), 4: (1, 3)}[Y]
    RING, BACK = cfg.RING, cfg.BACK
    g, e = lax.axis_index("group"), lax.axis_index("ep")
    zh, x = g // X, g % X
    z, me = e // E, e % E
    y, k = me // K, me % K

    def plane(peer):
        return (g, z * E + peer)

    def ypeer(dy):
        return ((y + dy) % Y) * K + k

    sib = y * K + (K - 1 - k)
    left, right = (g, e - E), (g, e + E)

    def xpeer(dx):
        return (zh * X + (x + dx) % X, e)

    partner = ((ZH - 1 - zh) * X + x, e)

    def rcopy(src, dst, ss, rs, dev):
        return pltpu.make_async_remote_copy(
            src_ref=src, dst_ref=dst, send_sem=ss, recv_sem=rs, device_id=dev, device_id_type=MESH
        )

    def cols(j):
        return pl.ds(pl.multiple_of(j * HC, HC), HC)

    def load_master(j):
        return pltpu.make_async_copy(master.at[:, cols(j)], mv.at[j], msem.at[j])

    def load_mom1(j):
        return pltpu.make_async_copy(mom1.at[:, cols(j)], v1.at[j], v1sem.at[j])

    def load_mom2(j):
        return pltpu.make_async_copy(mom2.at[:, cols(j)], v2.at[j], v2sem.at[j])

    def store_master(j):
        return pltpu.make_async_copy(mv.at[j], master_out.at[:, cols(j)], mosem.at[j])

    def store_mom1(j):
        return pltpu.make_async_copy(v1.at[j], mom1_out.at[:, cols(j)], o1sem.at[j])

    def store_mom2(j):
        return pltpu.make_async_copy(v2.at[j], mom2_out.at[:, cols(j)], o2sem.at[j])

    load_feat = pltpu.make_async_copy(feat, fv, lsem.at[0])
    load_grads = pltpu.make_async_copy(grads, uv, lsem.at[1])
    load_feat.start()
    load_grads.start()
    for j in range(NCH):
        load_master(j).start()

    barrier = pltpu.get_barrier_semaphore()

    def greet(dev):
        pl.semaphore_signal(barrier, inc=1, device_id=dev, device_id_type=MESH)

    for d in range(1, E):
        greet(plane((me + d) % E))
    for dx in range(1, X):
        greet(xpeer(dx))
    if ZH > 1:
        greet(partner)

    @pl.when(z > 0)
    def _():
        greet(left)

    @pl.when(z < LAST)
    def _():
        greet(right)

    marks = [
        jnp.where(slots[r:r + 1, :] == c, 1.0, 0.0) for c in range(SLOTS) for r in range(2)
    ]
    marks = jnp.concatenate(
        marks + [gates[...], jnp.zeros((128 - 2 * SLOTS - 2, T), F32)], axis=0
    )
    wide = -T % 128
    if wide:
        marks = jnp.concatenate([marks, jnp.zeros((128, wide), F32)], axis=1)
    gm[...] = marks.T[:T]

    PWL = fs.shape[2]
    tail = gm[:, :PWL - PW].astype(BF16)
    load_feat.wait()
    for d in range(E):
        fs[d] = jnp.concatenate([fv[:, d * PW:(d + 1) * PW], tail], axis=1)

    def scale(j):
        for r in range(2):
            gate = gm[:, 2 * SLOTS + r:2 * SLOTS + r + 1]
            sall[j, me, r] = (uv[:, r, cols(j)].astype(F32) * gate).astype(BF16)

    def weights(j):
        load_master(j).wait()
        wall[j, z] = mv[j].astype(BF16)

    load_grads.wait()
    scale(0)
    weights(0)

    pl.semaphore_wait(
        barrier,
        E - 1 + X - 1 + ZH - 1
        + jnp.where(z > 0, 1, 0) + jnp.where(z < LAST, 1, 0),
    )

    def y_copy(j, dy):
        return rcopy(sall.at[j, me], sall.at[j, me], ysend.at[j, dy], yrecv.at[j, dy], plane(ypeer(dy)))

    def y_from(j, dy):
        src = sall.at[j, ypeer(-dy)]
        return rcopy(src, src, ysend.at[j, dy], yrecv.at[j, dy], plane(ypeer(dy)))

    def c_copy(j, dy):
        src = sall.at[j, ypeer(-dy)]
        return rcopy(src, src, csend.at[j, dy], crecv.at[j, dy], plane(sib))

    def c_from(j, dy):
        src = sall.at[j, ((y - dy) % Y) * K + (K - 1 - k)]
        return rcopy(src, src, csend.at[j, dy], crecv.at[j, dy], plane(sib))

    def h_copy(j, dy):
        h = 0 if dy == 1 else 1
        src = sall.at[j, ypeer(-dy), h]
        return rcopy(src, src, hsend.at[j, h], hrecv.at[j, h], plane(ypeer(dy)))

    def h_from(j, h):
        src = sall.at[j, ypeer(2), h]
        return rcopy(src, src, hsend.at[j, h], hrecv.at[j, h], plane(ypeer(1)))

    def o_copy(j, h):
        src = sall.at[j, ypeer(2), h]
        return rcopy(src, src, osend.at[j, h], orecv.at[j, h], plane(sib))

    def o_from(j, h):
        src = sall.at[j, ((y + 2) % Y) * K + (K - 1 - k), h]
        return rcopy(src, src, osend.at[j, h], orecv.at[j, h], plane(sib))

    def f_copy(d):
        peer = (me + d) % E
        return rcopy(fs.at[peer], fall.at[me], fsend.at[d], frecv.at[d], plane(peer))

    def f_from(d):
        src = fall.at[(me - d) % E]
        return rcopy(src, src, fsend.at[d], frecv.at[d], plane((me + d) % E))

    def b_copy(d):
        peer = (me + d) % E
        return rcopy(bs.at[peer], br.at[me], bsend.at[d], brecv.at[d], plane(peer))

    def b_from(d):
        src = br.at[(me - d) % E]
        return rcopy(src, src, bsend.at[d], brecv.at[d], plane((me + d) % E))

    def w_right(j, s, slot):
        return rcopy(wall.at[j, slot], wall.at[j, slot], wrs.at[j, s], wrr.at[j, s], right)

    def w_left(j, s, slot):
        return rcopy(wall.at[j, slot], wall.at[j, slot], wls.at[j, s], wlr.at[j, s], left)

    def w_from_left(j, s, slot):
        return rcopy(wall.at[j, slot], wall.at[j, slot], wrs.at[j, s], wrr.at[j, s], left)

    def w_from_right(j, s, slot):
        return rcopy(wall.at[j, slot], wall.at[j, slot], wls.at[j, s], wlr.at[j, s], right)

    def p_right(j, c):
        return rcopy(ks.at[j, c], rl.at[j, c - 1], prs.at[j, c], prr.at[j, c], right)

    def p_left(j, c):
        return rcopy(ks.at[j, c], rr.at[j, c], pls.at[j, c], plr.at[j, c], left)

    def p_from_left(j, c):
        return rcopy(rl.at[j, c - 1], rl.at[j, c - 1], prs.at[j, c], prr.at[j, c], left)

    def p_from_right(j, c):
        return rcopy(rr.at[j, c], rr.at[j, c], pls.at[j, c], plr.at[j, c], right)

    def xrows(who):
        return pl.ds(pl.multiple_of(who * XR, 16), XR)

    def x1_copy(j, dx):
        return rcopy(
            part.at[j, :, xrows((x + dx) % X)], x1r.at[j, x],
            x1ss.at[j, dx], x1rs.at[j, dx], xpeer(dx),
        )

    def x1_from(j, dx):
        src = x1r.at[j, (x - dx) % X]
        return rcopy(src, src, x1ss.at[j, dx], x1rs.at[j, dx], xpeer(dx))

    def z_copy(j):
        return rcopy(zs.at[j], zr.at[j], zss.at[j], zrs.at[j], partner)

    def x2_copy(j, dx):
        return rcopy(
            x2s.at[j, dx], g2.at[j, xrows(x)], x2ss.at[j, dx], x2rs.at[j, dx], xpeer(dx)
        )

    def x2_from(j, dx):
        src = g2.at[j, xrows((x - dx) % X)]
        return rcopy(src, src, x2ss.at[j, dx], x2rs.at[j, dx], xpeer(dx))

    def send_scaled(j):
        for dy in near:
            y_copy(j, dy).start()
        if K > 1:
            c_copy(j, 0).start()

    def send_weights(j):
        @pl.when(z < LAST)
        def _():
            w_right(j, 0, z).start()

        @pl.when(z > 0)
        def _():
            w_left(j, 0, z).start()

    def pass_weights(j, s):
        zm = LAST - z

        @pl.when(z >= s)
        def _():
            w_from_left(j, s - 1, z - s).wait_recv()

        @pl.when((z >= s) & (z < LAST))
        def _():
            w_right(j, s, z - s).start()

        @pl.when(zm >= s)
        def _():
            w_from_right(j, s - 1, z + s).wait_recv()

        @pl.when((zm >= s) & (z > 0))
        def _():
            w_left(j, s, z + s).start()

    def when_chunk(i, lag, f):
        j = i - lag

        @pl.when((j >= 0) & (j < NCH))
        def _():
            f(j)

    def gather_near(j):
        for dy in near:
            y_from(j, dy).wait_recv()
            if Y == 4:
                h_copy(j, dy).start()
            if K > 1:
                c_copy(j, dy).start()

    def gather_far(j):
        if Y == 4:
            for h in range(2):
                h_from(j, h).wait_recv()
                if K > 1:
                    o_copy(j, h).start()

    def partials(j, ring):
        def pick(b, _):
            for c in range(SLOTS):
                m0 = mb[b, :, (2 * c) * 128:(2 * c + 1) * 128]
                m1 = mb[b, :, (2 * c + 1) * 128:(2 * c + 2) * 128]
                for l in range(HC // 128):
                    ln = slice(l * 128, (l + 1) * 128)
                    pk[ring, c, b, :, ln] = (
                        sall[j, b, 0, :, ln] * m0 + sall[j, b, 1, :, ln] * m1
                    )
            return 0

        lax.fori_loop(0, E, pick, 0)

        def one(c, _):
            part[j, c] = jnp.dot(
                ft[...], pk[ring, c].reshape(E * T, HC), preferred_element_type=F32
            ).astype(BF16)
            return 0

        lax.fori_loop(0, SLOTS, one, 0)

    def kind_of(who, c):
        return jnp.where(place[c, zh * X + who] >= KIND, 1.0, 0.0).astype(F32)

    def kind_sums(j):
        for dx in range(1, X):
            x1_from(j, dx).wait_recv()

        def one(c, _):
            own = part[j, c, xrows(x)].astype(F32)
            weight = kind_of(x, c)
            second = own * weight
            total = own
            for dx in range(1, X):
                who = (x - dx) % X
                got = x1r[j, who, c].astype(F32)
                second += got * kind_of(who, c)
                total += got
            ks[j, c, 0] = (total - second).astype(BF16)
            ks[j, c, 1] = second.astype(BF16)
            return 0

        lax.fori_loop(0, SLOTS, one, 0)

    def reduce_stage(j, s):
        @pl.when(z == s)
        def _():
            for c in range(LAST, s, -1):
                if s > 0:
                    p_from_left(j, c).wait_recv()
                    ks[j, c] = (ks[j, c].astype(F32) + rl[j, c - 1].astype(F32)).astype(BF16)
                p_right(j, c).start()

        @pl.when(z == LAST - s)
        def _():
            for c in range(0, LAST - s):
                if s > 0:
                    p_from_right(j, c).wait_recv()
                    ks[j, c] = (ks[j, c].astype(F32) + rr[j, c].astype(F32)).astype(BF16)
                p_left(j, c).start()

    def finish(j):
        for zz in range(SLOTS):
            @pl.when(z == zz)
            def _(zz=zz):
                total = ks[j, zz].astype(F32)
                if zz > 0:
                    p_from_left(j, zz).wait_recv()
                    total = total + rl[j, zz - 1].astype(F32)
                if zz < LAST:
                    p_from_right(j, zz).wait_recv()
                    total = total + rr[j, zz].astype(F32)
                zs[j] = total.astype(BF16)

        if ZH > 1:
            z_copy(j).start()

    def spread(j):
        zero, one = zs[j, 0].astype(F32), zs[j, 1].astype(F32)
        if ZH > 1:
            z_copy(j).wait_recv()
            zero += zr[j, 0].astype(F32)
            one += zr[j, 1].astype(F32)
        for dx in range(X):
            weight = kind_of((x + dx) % X, z)
            chosen = (one * weight + zero * (1.0 - weight)).astype(BF16)
            if dx == 0:
                g2[j, xrows(x)] = chosen
            else:
                x2s[j, dx] = chosen
                x2_copy(j, dx).start()

    def collect(j):
        for dx in range(1, X):
            x2_from(j, dx).wait_recv()
        load_mom1(j).wait()
        load_mom2(j).wait()

        def update(b, _):
            rows = xrows(b)
            gradient = g2[j, rows].astype(F32) * grad_scale
            first = beta_one * v1[j, rows].astype(F32) + (1.0 - beta_one) * gradient
            second = beta_two * v2[j, rows].astype(F32) + (1.0 - beta_two) * gradient * gradient
            change = (
                first
                / (1.0 - beta_one**10)
                / (jnp.sqrt(second / (1.0 - beta_two**10)) + epsilon)
            )
            old = mv[j, rows]
            mv[j, rows] = old - learn_rate * (change + decay_rate * old)
            v1[j, rows] = first.astype(BF16)
            v2[j, rows] = second.astype(BF16)
            return 0

        lax.fori_loop(0, X, update, 0)
        store_master(j).start()
        store_mom1(j).start()
        store_mom2(j).start()

    def back(j, ring):
        pass_weights(j, 3)

        def block(b, _):
            total = ba[b]
            for c in range(SLOTS):
                total += lax.dot_general(
                    pk[ring, c, b], wall[j, c], (((1,), (1,)), ((), ())),
                    preferred_element_type=F32,
                )
            ba[b] = total
            return 0

        lax.fori_loop(0, E, block, 0)

    for d in range(1, E):
        f_copy(d).start()
    send_scaled(0)
    send_weights(0)

    def prepare(j, _):
        scale(j)
        weights(j)

        send_weights(j)
        load_mom1(j).start()
        load_mom2(j).start()
        return 0

    load_mom1(0).start()
    load_mom2(0).start()
    lax.fori_loop(1, NCH, prepare, 0)
    fall[me] = fs[me]

    def clear(b, _):
        ba[b] = jnp.zeros((T, PW), F32)
        return 0

    lax.fori_loop(0, E, clear, 0)

    for j in range(NCH // 2):
        pass_weights(j, 1)
    gather_near(0)
    send_scaled(1)
    gather_far(0)
    for j in range(NCH // 2, NCH):
        pass_weights(j, 1)
    for d in range(1, E):
        f_from(d).wait_recv()

    first = (PW // 128) * 128
    spot = lax.broadcasted_iota(jnp.int32, (128, 2 * SLOTS * 128), 0)
    lane = lax.broadcasted_iota(jnp.int32, (128, 2 * SLOTS * 128), 1)
    pick_lane = jnp.where(spot - (PW - first) == lane // 128, 1.0, 0.0).astype(BF16)

    def masks(b, _):
        mb[b] = jnp.dot(
            fall[b, :, first:first + 128], pick_lane, preferred_element_type=F32
        ).astype(BF16)
        return 0

    lax.fori_loop(0, E, masks, 0)
    ft[...] = fall[...].reshape(E * T, fall.shape[2]).T[:PW]

    def step(i, _):
        when_chunk(i, -2, send_scaled)
        when_chunk(i, -1, gather_near)
        when_chunk(2 * i, 0, lambda j: pass_weights(j, 2))
        when_chunk(2 * i + 1, 0, lambda j: pass_weights(j, 2))

        def sums(j):
            kind_sums(j)
            reduce_stage(j, 0)


        def compute(j):
            if K > 1:
                for dy in (0, *near):
                    c_from(j, dy).wait_recv()
                if Y == 4:
                    for h in range(2):
                        o_from(j, h).wait_recv()
            partials(j, j % RING)
            for dx in range(1, X):
                x1_copy(j, dx).start()

        when_chunk(i, 0, compute)
        when_chunk(i, -1, gather_far)
        when_chunk(i, 1, sums)
        when_chunk(i, 2, lambda j: reduce_stage(j, 1))
        when_chunk(i, 3, lambda j: reduce_stage(j, 2))
        when_chunk(i, 4, finish)
        when_chunk(i, 5, spread)
        when_chunk(i, 6, collect)
        when_chunk(i, BACK, lambda j: back(j, j % RING))

        @pl.when(i == NCH - 1 + BACK)
        def _():
            def out(b, _):
                bs[b, :, :PW] = ba[b].astype(BF16)
                return 0

            lax.fori_loop(0, E, out, 0)
            for d in range(1, E):
                b_copy(d).start()

        return 0

    lax.fori_loop(0, NCH + 7, step, 0)

    br[me] = bs[me]
    for d in range(1, E):
        b_from(d).wait_recv()
    for d in range(E):
        ig_out[:, d * PW:(d + 1) * PW] = br[d, :, :PW]

    for d in range(1, E):
        f_copy(d).wait_send()
        b_copy(d).wait_send()

    def drain(j, _):
        for dy in near:
            y_copy(j, dy).wait_send()
            if Y == 4:
                h_copy(j, dy).wait_send()
        if K > 1:
            for dy in (0, *near):
                c_copy(j, dy).wait_send()
            if Y == 4:
                for h in range(2):
                    o_copy(j, h).wait_send()
        for s in range(SLOTS - 1):
            @pl.when((z >= s) & (z < LAST))
            def _(s=s):
                w_right(j, s, z - s).wait_send()

            @pl.when((LAST - z >= s) & (z > 0))
            def _(s=s):
                w_left(j, s, z + s).wait_send()

            @pl.when(z == s)
            def _(s=s):
                for c in range(LAST, s, -1):
                    p_right(j, c).wait_send()

            @pl.when(z == LAST - s)
            def _(s=s):
                for c in range(0, LAST - s):
                    p_left(j, c).wait_send()

        for dx in range(1, X):
            x1_copy(j, dx).wait_send()
            x2_copy(j, dx).wait_send()
        if ZH > 1:
            z_copy(j).wait_send()
        store_master(j).wait()
        store_mom1(j).wait()
        store_mom2(j).wait()
        return 0

    lax.fori_loop(0, NCH, drain, 0)


def on_device(
    cfg, activations, up_grad, gate_weights, route_slot, placement, master, moment_one, moment_two
):
    X, Y, K, T, PW, NCH, HC = cfg.X, cfg.Y, cfg.K, cfg.T, cfg.PW, cfg.NCH, cfg.HC
    E = Y * K
    PWL = PW + -PW % 128
    XR = PW // X
    DMA = pltpu.SemaphoreType.DMA
    vm = pl.BlockSpec(memory_space=pltpu.VMEM)
    sm = pl.BlockSpec(memory_space=pltpu.SMEM)
    hbm = pl.BlockSpec(memory_space=pl.ANY)

    def sems(*shape):
        return [DMA(shape), DMA(shape)]

    outs = pl.pallas_call(
        functools.partial(kernel, cfg),
        out_shape=(
            jax.ShapeDtypeStruct((T, E * PW), BF16),
            jax.ShapeDtypeStruct((PW, NCH * HC), F32),
            jax.ShapeDtypeStruct((PW, NCH * HC), BF16),
            jax.ShapeDtypeStruct((PW, NCH * HC), BF16),
        ),
        in_specs=[hbm, hbm, vm, vm, sm, hbm, hbm, hbm],
        out_specs=(vm, hbm, hbm, hbm),
        scratch_shapes=[
            pltpu.VMEM((T, E * PW), BF16),
            pltpu.VMEM((T, 2, NCH * HC), BF16),
            pltpu.VMEM((NCH, PW, HC), F32),
            pltpu.VMEM((NCH, PW, HC), BF16),
            pltpu.VMEM((NCH, PW, HC), BF16),
            pltpu.VMEM((T, 128), F32),
            pltpu.VMEM((E, T, PWL), BF16),
            pltpu.VMEM((NCH, SLOTS, PW, HC), BF16),
            pltpu.VMEM((E, T, PWL), BF16),
            pltpu.VMEM((PW, E * T), BF16),
            pltpu.VMEM((E, T, 2 * SLOTS * 128), BF16),
            pltpu.VMEM((NCH, E, 2, T, HC), BF16),
            pltpu.VMEM((cfg.RING, SLOTS, E, T, HC), BF16),
            pltpu.VMEM((NCH, SLOTS, PW, HC), BF16),
            pltpu.VMEM((NCH, SLOTS, 2, XR, HC), BF16),
            pltpu.VMEM((NCH, SLOTS - 1, 2, XR, HC), BF16),
            pltpu.VMEM((NCH, SLOTS - 1, 2, XR, HC), BF16),
            pltpu.VMEM((NCH, X, SLOTS, XR, HC), BF16),
            pltpu.VMEM((NCH, 2, XR, HC), BF16),
            pltpu.VMEM((NCH, 2, XR, HC), BF16),
            pltpu.VMEM((NCH, X, XR, HC), BF16),
            pltpu.VMEM((NCH, PW, HC), BF16),
            pltpu.VMEM((E, T, PW), F32),
            pltpu.VMEM((E, T, PWL), BF16),
            pltpu.VMEM((E, T, PWL), BF16),
            *sems(NCH, Y), *sems(NCH, 2), *sems(NCH, Y), *sems(NCH, 2), *sems(E), *sems(E),
            *sems(NCH, SLOTS), *sems(NCH, SLOTS), *sems(NCH, SLOTS), *sems(NCH, SLOTS),
            *sems(NCH, X), *sems(NCH), *sems(NCH, X),
            DMA((2,)), *sems(NCH), *sems(NCH), *sems(NCH),
        ],
        compiler_params=pltpu.CompilerParams(
            collective_id=0, has_side_effects=True, vmem_limit_bytes=63 << 20
        ),
        name="exchange",
    )(
        activations, up_grad, gate_weights.T, route_slot.T, placement.T,
        master[0], moment_one[0], moment_two[0],
    )
    return outs[0], outs[1][None], outs[2][None], outs[3][None]


def solution(mesh, cfg=FULL):
    in_specs = (
        P(("group", "ep"), None),
        P(("group", "ep"), None, None),
        P(("group", "ep"), None),
        P(("group", "ep"), None),
        P(),
        P("group", "ep", None),
        P("group", "ep", None),
        P("group", "ep", None),
    )
    out_specs = (
        P(("group", "ep"), None),
        P("group", "ep", None),
        P("group", "ep", None),
        P("group", "ep", None),
    )
    return jax.shard_map(
        functools.partial(on_device, cfg),
        mesh=mesh, in_specs=in_specs, out_specs=out_specs, check_vma=False,
    )
```

time: 173 us -> 137 us (0.79); the launches traced: 170 us -> 137 us
  Pallas kernels: 149 us -> 130 us
  other arithmetic: 9.63 us -> 0 us
  local copies, waits for them, and re-layouts: 10 us -> 6.13 us
    pallas_call x1, Pallas kernels: 149 us -> 130 us  [on_device(): pl.pallas_call(functools.partial(kernel, cfg), out_shape=(jax.ShapeDtypeS...]
    broadcast_in_dim x1 -> x0, other arithmetic: 6.01 us -> none  [on_device(): second_moment.astype(BF16)[None]]
    reshape x5 -> x0, local copies, waits for them, and re-layouts: 4.82 us -> none  [the longest x2 2.23 us: on_device(): scl = scaled.reshape(T, 2, NCH, HC).transpose(2, 1, 0, 3)]
    unnamed x6 -> x10, local copies, waits for them, and re-layouts: 2.16 us -> 6.13 us
    convert_element_type x1 -> x0, other arithmetic: 2.26 us -> none  [on_device(): scaled = (gate_weights[:, :, None] * up_grad.astype(F32)).astype(BF16)]
    transpose x1 -> x0, local copies, waits for them, and re-layouts: 2.1 us -> none  [on_device(): input_grad = back.transpose(1, 0, 2).reshape(T, E * PW)]
where the time goes in v2:
time: 137 us
  Pallas kernels  130 us (95%)
  local copies, waits for them, and re-layouts  6.13 us (4%)
    pallas_call x1, Pallas kernels, on_device(): pl.pallas_call(functools.partial(kernel, cfg), out_shape=(jax.ShapeDtypeS...  130 us
    unnamed x10, local copies, waits for them, and re-layouts  6.13 us

profile of v2, /device:TPU:6, one launch (start us, length us, event | category | flops | bytes accessed | tf_op | source)
XLA Modules:
  0.0 137.0 jit_solution(10032620938045670450)
XLA Ops:
  0.6 130.2 %exchange.1 = (bf16[192,2560]{1,0:T(8,128)(2,1)}, f32[320,1536]{1,0:T(8,128)}, bf16[320,1536]{1,0:T(8,128)(2,1)}, bf16[320,1536]{1,0:T(8,128)(2,1)}) custom-call(bf16[192,2560]{1,0:T(8,128)(2,1)} %feat.1, bf16[192,2,1536]{2,1,0:T(2,128)(2,1)} %grads.1, f32[2,192]{1,0:T(2,128)} %bitcast.15, s32[2,192]{1,0:T(2,128)} %bitcast.16, s32[4,8]{1,0:T(4,128)} %bitcast.17, ...), custom_call_target="tpu_custom_call" | custom-call | tf_op jit(solution)/shard_map/exchange/pallas_call | solution.py:605
  130.9 0.0 copy-start
  130.9 2.4 %copy.16 = bf16[192,2560]{1,0:T(8,128)(2,1)} copy(bf16[192,2560]{1,0:T(8,128)(2,1)} %get-tuple-element.16) | data formatting | bytes 1966080
  133.2 0.0 copy-done
  133.2 0.0 copy-start.2
  133.2 0.0 copy-start.1
  133.3 1.3 copy.17
  134.5 0.6 copy-done.2
  135.1 0.9 copy.18
  136.1 0.0 copy-done.1
  136.1 0.9 copy.19
Async XLA Ops:
  130.9 2.4 %copy-start = (f32[320,1536]{1,0:T(8,128)S(1)}, f32[320,1536]{1,0:T(8,128)}, u32[]{:S(2)}) copy-start(f32[320,1536]{1,0:T(8,128)} %get-tuple-element.9) | copy-start | bytes 5898244
  133.2 1.9 %copy-start.2 = (bf16[320,1536]{1,0:T(8,128)(2,1)S(1)}, bf16[320,1536]{1,0:T(8,128)(2,1)}, u32[]{:S(2)}) copy-start(bf16[320,1536]{1,0:T(8,128)(2,1)} %get-tuple-element.10) | copy-start | bytes 2949124
  133.2 2.8 %copy-start.1 = (bf16[320,1536]{1,0:T(8,128)(2,1)S(1)}, bf16[320,1536]{1,0:T(8,128)(2,1)}, u32[]{:S(2)}) copy-start(bf16[320,1536]{1,0:T(8,128)(2,1)} %get-tuple-element.11) | copy-start | bytes 2949124

commit v3 on v2

--- a/solution.py
+++ b/solution.py
@@ -22,7 +22,7 @@
 F32 = jnp.float32
 BF16 = jnp.bfloat16
 
-FULL = SimpleNamespace(ZH=2, X=4, Y=4, K=2, T=192, PW=320, NCH=6, HC=256, RING=3, BACK=2)
+FULL = SimpleNamespace(ZH=2, X=4, Y=4, K=2, T=192, PW=320, NCH=6, HC=256, RING=3, BACK=2, EARLY=2, LAGS=(1, 2, 3, 4, 6, 7))
 
 
 def kernel(
@@ -141,10 +141,6 @@
         load_master(j).wait()
         wall[j, z] = mv[j].astype(BF16)
 
-    load_grads.wait()
-    scale(0)
-    weights(0)
-
     pl.semaphore_wait(
         barrier,
         E - 1 + X - 1 + ZH - 1
@@ -441,21 +437,22 @@
 
     for d in range(1, E):
         f_copy(d).start()
-    send_scaled(0)
-    send_weights(0)
-
-    def prepare(j, _):
+
+    def first_weights(j, _):
+        weights(j)
+        send_weights(j)
+        return 0
+
+    lax.fori_loop(0, NCH, first_weights, 0)
+    load_grads.wait()
+
+    def scale_all(j, _):
         scale(j)
-        weights(j)
-
-        send_weights(j)
         load_mom1(j).start()
         load_mom2(j).start()
         return 0
 
-    load_mom1(0).start()
-    load_mom2(0).start()
-    lax.fori_loop(1, NCH, prepare, 0)
+    lax.fori_loop(0, NCH, scale_all, 0)
     fall[me] = fs[me]
 
     def clear(b, _):
@@ -463,14 +460,9 @@
         return 0
 
     lax.fori_loop(0, E, clear, 0)
-
-    for j in range(NCH // 2):
+    for j in range(cfg.EARLY):
         pass_weights(j, 1)
-    gather_near(0)
-    send_scaled(1)
-    gather_far(0)
-    for j in range(NCH // 2, NCH):
-        pass_weights(j, 1)
+    send_scaled(0)
     for d in range(1, E):
         f_from(d).wait_recv()
 
@@ -487,6 +479,13 @@
 
     lax.fori_loop(0, E, masks, 0)
     ft[...] = fall[...].reshape(E * T, fall.shape[2]).T[:PW]
+    gather_near(0)
+    send_scaled(1)
+    gather_far(0)
+    for j in range(cfg.EARLY, NCH):
+        pass_weights(j, 1)
+
+    lags = cfg.LAGS
 
     def step(i, _):
         when_chunk(i, -2, send_scaled)
@@ -512,12 +511,12 @@
 
         when_chunk(i, 0, compute)
         when_chunk(i, -1, gather_far)
-        when_chunk(i, 1, sums)
-        when_chunk(i, 2, lambda j: reduce_stage(j, 1))
-        when_chunk(i, 3, lambda j: reduce_stage(j, 2))
-        when_chunk(i, 4, finish)
-        when_chunk(i, 5, spread)
-        when_chunk(i, 6, collect)
+        when_chunk(i, lags[0], sums)
+        when_chunk(i, lags[1], lambda j: reduce_stage(j, 1))
+        when_chunk(i, lags[2], lambda j: reduce_stage(j, 2))
+        when_chunk(i, lags[3], finish)
+        when_chunk(i, lags[4], spread)
+        when_chunk(i, lags[5], collect)
         when_chunk(i, BACK, lambda j: back(j, j % RING))
 
         @pl.when(i == NCH - 1 + BACK)
@@ -532,7 +531,7 @@
 
         return 0
 
-    lax.fori_loop(0, NCH + 7, step, 0)
+    lax.fori_loop(0, NCH + lags[5], step, 0)
 
     br[me] = bs[me]
     for d in range(1, E):
@@ -585,6 +584,42 @@
         return 0
 
     lax.fori_loop(0, NCH, drain, 0)
+
+
+def hand_out(arrays):
+    parts = 4
+    count = len(arrays)
+
+    def body(*refs):
+        held, load, store = refs[2 * count:3 * count], refs[-2], refs[-1]
+        moves = []
+        for n in range(count):
+            rows = arrays[n].shape[0] // parts
+            for p in range(parts):
+                cut = pl.ds(p * rows, rows)
+                moves.append((
+                    pltpu.make_async_copy(refs[n].at[cut], held[n].at[cut], load.at[n, p]),
+                    pltpu.make_async_copy(held[n].at[cut], refs[count + n].at[cut], store.at[n, p]),
+                ))
+        for first, _ in moves:
+            first.start()
+        for first, second in moves:
+            first.wait()
+            second.start()
+        for _, second in moves:
+            second.wait()
+
+    hbm = pl.BlockSpec(memory_space=pl.ANY)
+    sems = pltpu.SemaphoreType.DMA((count, parts))
+    return pl.pallas_call(
+        body,
+        out_shape=[jax.ShapeDtypeStruct(a.shape, a.dtype) for a in arrays],
+        in_specs=[hbm] * count,
+        out_specs=[hbm] * count,
+        scratch_shapes=[*[pltpu.VMEM(a.shape, a.dtype) for a in arrays], sems, sems],
+        compiler_params=pltpu.CompilerParams(vmem_limit_bytes=63 << 20),
+        name="hand_out",
+    )(*arrays)
 
 
 def on_device(
@@ -651,6 +686,7 @@
         activations, up_grad, gate_weights.T, route_slot.T, placement.T,
         master[0], moment_one[0], moment_two[0],
     )
+    outs = hand_out(outs)
     return outs[0], outs[1][None], outs[2][None], outs[3][None]
 
 

time: 137 us -> 136 us (level); the launches traced: 137 us -> 134 us
  local copies, waits for them, and re-layouts: 6.13 us -> 0 us
  Pallas kernels: 130 us -> 134 us
    unnamed x10 -> x0, local copies, waits for them, and re-layouts: 6.13 us -> none
    pallas_call x0 -> x1, Pallas kernels: none -> 4.8 us  [hand_out(): pl.pallas_call(body, out_shape=[jax.ShapeDtypeStruct(a.shape, a.dtype) fo...]
    pallas_call x1, Pallas kernels: 130 us -> 129 us  [on_device(): pl.pallas_call(functools.partial(kernel, cfg), out_shape=(jax.ShapeDtypeS...]
where the time goes in v3:
time: 136 us; the launch traced here: 134 us
  Pallas kernels  134 us (99%)
    pallas_call x1, Pallas kernels, on_device(): pl.pallas_call(functools.partial(kernel, cfg), out_shape=(jax.ShapeDtypeS...  129 us
    pallas_call x1, Pallas kernels, hand_out(): pl.pallas_call(body, out_shape=[jax.ShapeDtypeStruct(a.shape, a.dtype) fo...  4.8 us

profile of v3, /device:TPU:6, one launch (start us, length us, event | category | flops | bytes accessed | tf_op | source)
XLA Modules:
  0.0 134.3 jit_solution(6124286966966031297)
XLA Ops:
  0.6 128.8 %exchange.1 = (bf16[192,2560]{1,0:T(8,128)(2,1)}, f32[320,1536]{1,0:T(8,128)}, bf16[320,1536]{1,0:T(8,128)(2,1)}, bf16[320,1536]{1,0:T(8,128)(2,1)}) custom-call(bf16[192,2560]{1,0:T(8,128)(2,1)} %feat.1, bf16[192,2,1536]{2,1,0:T(2,128)(2,1)} %grads.1, f32[2,192]{1,0:T(2,128)} %bitcast.12, s32[2,192]{1,0:T(2,128)} %bitcast.13, s32[4,8]{1,0:T(4,128)} %bitcast.14, ...), custom_call_target="tpu_custom_call" | custom-call | tf_op jit(solution)/shard_map/exchange/pallas_call | solution.py:640
  129.5 4.8 %hand_out.1 = (bf16[192,2560]{1,0:T(8,128)(2,1)}, f32[320,1536]{1,0:T(8,128)}, bf16[320,1536]{1,0:T(8,128)(2,1)}, bf16[320,1536]{1,0:T(8,128)(2,1)}) custom-call(bf16[192,2560]{1,0:T(8,128)(2,1)} %get-tuple-element.12.refs_0_, f32[320,1536]{1,0:T(8,128)} %get-tuple-element.13.refs_1_, bf16[320,1536]{1,0:T(8,128)(2,1)} %get-tuple-element.14.refs_2_, ...), custom_call_target="tpu_custom_call" | custom-call | tf_op jit(solution)/shard_map/hand_out/pallas_call | solution.py:614

commit v4 on v3

--- a/solution.py
+++ b/solution.py
@@ -485,65 +485,7 @@
     for j in range(cfg.EARLY, NCH):
         pass_weights(j, 1)
 
-    lags = cfg.LAGS
-
-    def step(i, _):
-        when_chunk(i, -2, send_scaled)
-        when_chunk(i, -1, gather_near)
-        when_chunk(2 * i, 0, lambda j: pass_weights(j, 2))
-        when_chunk(2 * i + 1, 0, lambda j: pass_weights(j, 2))
-
-        def sums(j):
-            kind_sums(j)
-            reduce_stage(j, 0)
-
-
-        def compute(j):
-            if K > 1:
-                for dy in (0, *near):
-                    c_from(j, dy).wait_recv()
-                if Y == 4:
-                    for h in range(2):
-                        o_from(j, h).wait_recv()
-            partials(j, j % RING)
-            for dx in range(1, X):
-                x1_copy(j, dx).start()
-
-        when_chunk(i, 0, compute)
-        when_chunk(i, -1, gather_far)
-        when_chunk(i, lags[0], sums)
-        when_chunk(i, lags[1], lambda j: reduce_stage(j, 1))
-        when_chunk(i, lags[2], lambda j: reduce_stage(j, 2))
-        when_chunk(i, lags[3], finish)
-        when_chunk(i, lags[4], spread)
-        when_chunk(i, lags[5], collect)
-        when_chunk(i, BACK, lambda j: back(j, j % RING))
-
-        @pl.when(i == NCH - 1 + BACK)
-        def _():
-            def out(b, _):
-                bs[b, :, :PW] = ba[b].astype(BF16)
-                return 0
-
-            lax.fori_loop(0, E, out, 0)
-            for d in range(1, E):
-                b_copy(d).start()
-
-        return 0
-
-    lax.fori_loop(0, NCH + lags[5], step, 0)
-
-    br[me] = bs[me]
-    for d in range(1, E):
-        b_from(d).wait_recv()
-    for d in range(E):
-        ig_out[:, d * PW:(d + 1) * PW] = br[d, :, :PW]
-
-    for d in range(1, E):
-        f_copy(d).wait_send()
-        b_copy(d).wait_send()
-
-    def drain(j, _):
+    def drain(j):
         for dy in near:
             y_copy(j, dy).wait_send()
             if Y == 4:
@@ -578,12 +520,80 @@
             x2_copy(j, dx).wait_send()
         if ZH > 1:
             z_copy(j).wait_send()
+
+    def assemble():
+        br[me] = bs[me]
+        for d in range(1, E):
+            b_from(d).wait_recv()
+        for d in range(E):
+            ig_out[:, d * PW:(d + 1) * PW] = br[d, :, :PW]
+
+    lags = cfg.LAGS
+
+    def step(i, _):
+        when_chunk(i, -2, send_scaled)
+        when_chunk(i, -1, gather_near)
+        when_chunk(2 * i, 0, lambda j: pass_weights(j, 2))
+        when_chunk(2 * i + 1, 0, lambda j: pass_weights(j, 2))
+
+        def sums(j):
+            kind_sums(j)
+            reduce_stage(j, 0)
+
+
+        def compute(j):
+            if K > 1:
+                for dy in (0, *near):
+                    c_from(j, dy).wait_recv()
+                if Y == 4:
+                    for h in range(2):
+                        o_from(j, h).wait_recv()
+            partials(j, j % RING)
+            for dx in range(1, X):
+                x1_copy(j, dx).start()
+
+        when_chunk(i, 0, compute)
+        when_chunk(i, -1, gather_far)
+        when_chunk(i, lags[0], sums)
+        when_chunk(i, lags[1], lambda j: reduce_stage(j, 1))
+        when_chunk(i, lags[2], lambda j: reduce_stage(j, 2))
+        when_chunk(i, lags[3], finish)
+        when_chunk(i, lags[4], spread)
+        when_chunk(i, lags[5], drain)
+
+        @pl.when(i == NCH - 1 + lags[5])
+        def _():
+            assemble()
+
+        when_chunk(i, lags[5], collect)
+        when_chunk(i, BACK, lambda j: back(j, j % RING))
+
+        @pl.when(i == NCH - 1 + BACK)
+        def _():
+            def out(b, _):
+                bs[b, :, :PW] = ba[b].astype(BF16)
+                return 0
+
+            lax.fori_loop(0, E, out, 0)
+            for d in range(1, E):
+                b_copy(d).start()
+
+        return 0
+
+    lax.fori_loop(0, NCH + lags[5], step, 0)
+
+
+    for d in range(1, E):
+        f_copy(d).wait_send()
+        b_copy(d).wait_send()
+
+    def stored(j, _):
         store_master(j).wait()
         store_mom1(j).wait()
         store_mom2(j).wait()
         return 0
 
-    lax.fori_loop(0, NCH, drain, 0)
+    lax.fori_loop(0, NCH, stored, 0)
 
 
 def hand_out(arrays):

time: 136 us -> 136 us (level)
  no operation moved by 1% of the time
where the time goes in v4:
time: 136 us; the launch traced here: 134 us
  Pallas kernels  134 us (99%)
    pallas_call x1, Pallas kernels, on_device(): pl.pallas_call(functools.partial(kernel, cfg), out_shape=(jax.ShapeDtypeS...  129 us
    pallas_call x1, Pallas kernels, hand_out(): pl.pallas_call(body, out_shape=[jax.ShapeDtypeStruct(a.shape, a.dtype) fo...  4.8 us

profile of v4, /device:TPU:6, one launch (start us, length us, event | category | flops | bytes accessed | tf_op | source)
XLA Modules:
  0.0 134.1 jit_solution(4884789087108004227)
XLA Ops:
  0.6 128.7 %exchange.1 = (bf16[192,2560]{1,0:T(8,128)(2,1)}, f32[320,1536]{1,0:T(8,128)}, bf16[320,1536]{1,0:T(8,128)(2,1)}, bf16[320,1536]{1,0:T(8,128)(2,1)}) custom-call(bf16[192,2560]{1,0:T(8,128)(2,1)} %feat.1, bf16[192,2,1536]{2,1,0:T(2,128)(2,1)} %grads.1, f32[2,192]{1,0:T(2,128)} %bitcast.12, s32[2,192]{1,0:T(2,128)} %bitcast.13, s32[4,8]{1,0:T(4,128)} %bitcast.14, ...), custom_call_target="tpu_custom_call" | custom-call | tf_op jit(solution)/shard_map/exchange/pallas_call | solution.py:650
  129.3 4.8 %hand_out.1 = (bf16[192,2560]{1,0:T(8,128)(2,1)}, f32[320,1536]{1,0:T(8,128)}, bf16[320,1536]{1,0:T(8,128)(2,1)}, bf16[320,1536]{1,0:T(8,128)(2,1)}) custom-call(bf16[192,2560]{1,0:T(8,128)(2,1)} %get-tuple-element.12.refs_0_, f32[320,1536]{1,0:T(8,128)} %get-tuple-element.13.refs_1_, bf16[320,1536]{1,0:T(8,128)(2,1)} %get-tuple-element.14.refs_2_, ...), custom_call_target="tpu_custom_call" | custom-call | tf_op jit(solution)/shard_map/hand_out/pallas_call | solution.py:624
